TPU v7x, 32 devices: a whole 2x2x4 slice. The times are simulated.
32 devices in a mesh: row: 8 (over z, y), col: 4 (over x, core).
Axes of the slice: x: 2, y: 2, z: 4, core: 2. Of those that a mesh axis runs over, the one named last changes fastest.
Arguments:
- amplitudes_right: float32 [8, 2048], P(None, ('row', 'col')), may hold values from -5 to 5
- amplitudes_left: float32 [8, 2048], P(None, ('row', 'col')), may hold values from -7 to 7
- previous_right: float32 [8, 2048], P(None, ('row', 'col')), may hold values from -6 to 6
- previous_left: float32 [8, 2048], P(None, ('row', 'col')), may hold values from -6 to 6
- coupling: float32 [2, 8], replicated, may hold values from 0.2 to 1
- ladder: bfloat16 [2048, 2048], P('row', 'col'), may hold values from -1 to 5
Outputs:
- next_right: float32 [8, 2048], P(None, ('row', 'col'))
- next_left: float32 [8, 2048], P(None, ('row', 'col'))
- coefficients: float32 [3, 8], replicated
All inputs are finite; a program needn't handle non-finite values.
Results may differ from a plain program's by a relative error of at most 0.003.
Values may be sent and summed in bfloat16 or wider, within the bound.
A program may use at most 64 MiB of HBM per device.

v0:
```python
import functools

import jax
import jax.numpy as jnp
from jax import lax
from jax.experimental import pallas as pl
from jax.experimental.pallas import tpu as pltpu
from jax.sharding import PartitionSpec as P

LOGICAL = pl.DeviceIdType.LOGICAL
LANES = 128
UNROLL_MOST = 32
SMALLEST_SQUARE = 1e-12


def each(count, body):
    if count <= UNROLL_MOST:
        for i in range(count):
            body(i)
    else:
        lax.fori_loop(0, count, lambda i, carry: (body(i), carry)[1], 0)


def arrived(ref, count, sem):
    part = ref.at[pl.ds(0, count)]
    pltpu.make_async_copy(part, part, sem).wait()


def kernel(
    rows_count,
    cols_count,
    right_in,
    left_in,
    prev_right_in,
    prev_left_in,
    coupling_in,
    ladder_in,
    next_right_out,
    next_left_out,
    coefficients_out,
    vectors_own,
    coupling_own,
    ladder_own,
    ladder_turned,
    left_sent,
    mates_sent,
    right_got,
    left_got,
    mates_got,
    right_part,
    left_part,
    right_part_got,
    left_part_got,
    sums_sent,
    sums_got,
    load_sem,
    send_sem,
    recv_sem,
):
    devices = rows_count * cols_count
    depth, share = right_in.shape
    pack = LANES // share
    pairs_total = share * devices
    my_row = lax.axis_index("row")
    my_col = lax.axis_index("col")
    me = my_row * cols_count + my_col
    home_col = lax.div(me, rows_count)
    home_slot = lax.rem(me, rows_count)
    at_home = home_col == my_col

    groups = devices // pack
    my_group = lax.div(me, pack)
    my_sub = lax.rem(me, pack)
    loads = [
        pltpu.make_async_copy(src, dst, load_sem.at[i])
        for i, (src, dst) in enumerate(
            (
                (right_in, vectors_own.at[0]),
                (left_in, vectors_own.at[1]),
                (prev_right_in, vectors_own.at[2]),
                (prev_left_in, vectors_own.at[3]),
                (coupling_in, coupling_own),
                (ladder_in, ladder_own),
            )
        )
    ]
    row_start = my_row * cols_count

    def peer(i):
        return row_start + lax.rem(my_col + i + 1, cols_count)

    def holder(i):
        return my_col * rows_count + lax.rem(home_slot + i, rows_count)

    def user(i):
        return lax.rem(my_row + i, rows_count) * cols_count + home_col

    def unless_me(i, go):
        if i == 0:
            pl.when(jnp.logical_not(at_home))(go)
        else:
            go()

    barrier = pltpu.get_barrier_semaphore()

    def greet(device):
        pl.semaphore_signal(barrier, inc=1, device_id=device, device_id_type=LOGICAL)

    for i in range(cols_count - 1):
        greet(peer(i))
    for load in loads[:2]:
        load.start()
    for i in range(rows_count):
        unless_me(i, lambda: greet(holder(i)))
    for i in range(rows_count):
        unless_me(i, lambda: greet(user(i)))
    for load in loads[2:]:
        load.start()

    lane = lax.broadcasted_iota(jnp.int32, (depth, LANES), 1)
    sub = lax.broadcasted_iota(jnp.int32, (depth, LANES), 0)

    mine = lane // share == my_sub

    def spread(i):
        return jnp.where(mine, jnp.concatenate([vectors_own[i]] * pack, axis=1), 0.0)

    def to_lanes(columns):
        row = jnp.zeros((depth, LANES), jnp.float32)
        for i, column in enumerate(columns):
            row = row + jnp.where(lane == sub + i * depth, column, 0.0)
        return jnp.sum(row, axis=0, keepdims=True)

    def to_column(row, i):
        return jnp.sum(jnp.where(lane == sub + i * depth, row, 0.0), axis=1, keepdims=True)

    for load in loads[:2]:
        load.wait()
    right_own = spread(0)
    left_own = spread(1)
    mates_sent[0] = right_own
    left_sent[0] = left_own
    left_got[pl.ds(my_col, 1)] = left_own[None]

    @pl.when(at_home)
    def _():
        right_got[pl.ds(home_slot, 1)] = right_own[None]

    pl.semaphore_wait(barrier, 2 * rows_count + cols_count - 1 - 2 * at_home.astype(jnp.int32))

    def send(src, dst, sems, device):
        pltpu.make_async_remote_copy(
            src_ref=src,
            dst_ref=dst,
            send_sem=send_sem.at[sems],
            recv_sem=recv_sem.at[sems],
            device_id=device,
            device_id_type=LOGICAL,
        ).start()

    for i in range(cols_count - 1):
        send(left_sent.at[0], left_got.at[my_col], 1, peer(i))
    for i in (*range(1, rows_count), 0):
        unless_me(i, lambda: send(mates_sent.at[0], right_got.at[home_slot], 0, user(i)))

    for load in loads[2:]:
        load.wait()
    mates_sent[1] = spread(2)
    mates_sent[2] = spread(3)
    mates_got[pl.ds(my_sub, 1)] = mates_sent[...][None]
    coupling_row = coupling_own[...]
    near = lax.broadcasted_iota(jnp.int32, (depth, depth), 0) == lax.broadcasted_iota(
        jnp.int32, (depth, depth), 1
    )

    def coefficient(i):
        return jnp.sum(jnp.where(near, coupling_row[i : i + 1], 0.0), axis=1, keepdims=True)

    def joined(ref, count):
        return jnp.concatenate(
            [sum(ref[i * pack + j] for j in range(pack)) for i in range(count // pack)], axis=1
        )

    arrived(left_got, cols_count - 1, recv_sem.at[1])
    left_rows = joined(left_got, cols_count)
    left_terms = jnp.dot(
        left_rows.astype(jnp.bfloat16), ladder_own[...], preferred_element_type=jnp.float32
    )
    for i in range(rows_count // pack):
        left_part[i] = left_terms[:, i * LANES : (i + 1) * LANES]

    for i in (*range(1, rows_count), 0):
        chunk = lax.div(lax.rem(home_slot + i, rows_count), pack)
        unless_me(
            i, lambda: send(left_part.at[chunk], left_part_got.at[my_row], 2, holder(i))
        )

    for i in range(pack - 1):
        mate = me - my_sub + lax.rem(my_sub + i + 1, pack)
        send(mates_sent, mates_got.at[my_sub], 5, mate)
    ladder_turned[...] = ladder_own[...].T

    @pl.when(at_home)
    def _():
        left_part_got[pl.ds(my_row, 1)] = left_part[pl.ds(lax.div(home_slot, pack), 1)]
        arrived(right_got, rows_count - 1, recv_sem.at[0])

    @pl.when(jnp.logical_not(at_home))
    def _():
        arrived(right_got, rows_count, recv_sem.at[0])

    right_cols = joined(right_got, rows_count)
    right_terms = jnp.dot(
        right_cols.astype(jnp.bfloat16), ladder_turned[...], preferred_element_type=jnp.float32
    )
    for i in range(cols_count // pack):
        right_part[i] = right_terms[:, i * LANES : (i + 1) * LANES]

    for i in range(cols_count - 1):
        chunk = lax.div(lax.rem(my_col + i + 1, cols_count), pack)
        send(right_part.at[chunk], right_part_got.at[my_col], 3, peer(i))
    right_part_got[pl.ds(my_col, 1)] = right_part[pl.ds(lax.div(my_col, pack), 1)]

    def inner(first, second):
        return jnp.sum(first * second, axis=1, keepdims=True)

    def inverse(square):
        usable = square > SMALLEST_SQUARE
        return jnp.where(usable, 1.0 / jnp.where(usable, square, 1.0), 0.0)

    arrived(mates_got, pack - 1, recv_sem.at[5])
    right, prev_right, prev_left = (
        sum(mates_got[i, j] for i in range(pack)) for j in range(3)
    )
    first_col = my_col - my_sub
    left = sum(left_got[first_col + i] for i in range(pack))
    right_square = inner(right, right)
    left_square = inner(left, left)
    left_right = inner(left, right)
    right_inverse = inverse(right_square)
    left_inverse = inverse(left_square)

    arrived(right_part_got, cols_count - 1, recv_sem.at[3])
    image_right = jnp.sum(right_part_got[...], axis=0)
    alpha_part = inner(left, image_right)
    right_base = image_right - coefficient(1) * prev_right
    right_fit = inner(right_base, right) * right_inverse
    right_rest = right_base - right_fit * right

    @pl.when(at_home)
    def _():
        arrived(left_part_got, rows_count - 1, recv_sem.at[2])

    @pl.when(jnp.logical_not(at_home))
    def _():
        arrived(left_part_got, rows_count, recv_sem.at[2])

    left_base = jnp.sum(left_part_got[...], axis=0) - coefficient(0) * prev_left
    left_fit = inner(left_base, left) * left_inverse
    left_rest = left_base - left_fit * left

    sums_sent[...] = to_lanes(
        [
            alpha_part,
            right_fit,
            left_fit,
            inner(right_rest, right_rest),
            inner(right_rest, right),
            right_square,
            inner(left_rest, left_rest),
            inner(left_rest, left),
            left_square,
            inner(left_rest, right_rest),
            inner(left_rest, right),
            inner(left, right_rest),
            left_right,
        ]
    )
    low = my_group < groups // 2

    def far_first(i):
        down = groups - 1 - i
        down = down - (down <= my_group).astype(jnp.int32)
        up = i + (i >= my_group).astype(jnp.int32)
        return jnp.where(low, down, up) * pack + my_sub

    each(
        groups - 1,
        lambda i: send(sums_sent, sums_got.at[pl.ds(my_group, 1)], 4, far_first(i)),
    )
    sums_got[pl.ds(my_group, 1)] = sums_sent[...]

    arrived(right_got, rows_count - 1, send_sem.at[0])
    arrived(left_got, cols_count - 1, send_sem.at[1])
    arrived(left_part_got, rows_count - 1, send_sem.at[2])
    arrived(right_part_got, cols_count - 1, send_sem.at[3])
    arrived(mates_got, pack - 1, send_sem.at[5])

    @pl.when(jnp.logical_not(at_home))
    def _():
        arrived(right_got, 1, send_sem.at[0])
        arrived(left_part_got, 1, send_sem.at[2])

    arrived(sums_got, groups - 1, recv_sem.at[4])
    sums = sums_got[...]

    def value(i):
        return pltpu.roll(sums, LANES - i * depth, 1)

    def total(values):
        return jnp.sum(values, axis=0, keepdims=True) / pairs_total

    alpha_row = total(sums)
    right_off = value(1) - alpha_row
    left_off = value(2) - alpha_row
    right_norm = to_column(
        total(value(3) + right_off * (2.0 * value(4) + right_off * value(5))), 0
    )
    left_norm = to_column(total(value(6) + left_off * (2.0 * value(7) + left_off * value(8))), 0)
    omega_val = to_column(
        total(
            value(9)
            + right_off * value(10)
            + left_off * value(11)
            + right_off * left_off * value(12)
        ),
        0,
    )
    alpha_now = to_column(alpha_row, 0)
    right_res = right_base - alpha_now * right
    left_res = left_base - alpha_now * left
    safe_omega = jnp.maximum(jnp.abs(omega_val), 0.1 * jnp.sqrt(right_norm * left_norm + 1e-06))
    beta_new = jnp.sqrt(safe_omega)
    gamma_new = omega_val / beta_new

    def own_part(array):
        out = array[:, :share]
        for i in range(1, pack):
            out = jnp.where(
                my_sub == i, array[:, i * share : (i + 1) * share], out
            )
        return out

    next_right_out[...] = own_part(right_res / beta_new)
    next_left_out[...] = own_part(left_res * (gamma_new / safe_omega))
    coefficients_out[0:1] = alpha_row[:, :depth]
    coefficients_out[1:2] = to_lanes([beta_new])[:, :depth]
    coefficients_out[2:3] = to_lanes([gamma_new])[:, :depth]
    arrived(sums_got, groups - 1, send_sem.at[4])


def store(a_in, b_in, c_in, a_out, b_out, c_out, sem):
    copies = [
        pltpu.make_async_copy(src, dst, sem.at[i])
        for i, (src, dst) in enumerate(((a_in, a_out), (b_in, b_out), (c_in, c_out)))
    ]
    for copy in copies:
        copy.start()
    for copy in copies:
        copy.wait()


def local(rows_count, cols_count, right, left, prev_right, prev_left, coupling, ladder):
    depth, share = right.shape
    devices = rows_count * cols_count
    pack = LANES // share
    f32 = jnp.float32

    def tiles(count):
        return pltpu.VMEM((count, depth, LANES), f32)

    results = pl.pallas_call(
        functools.partial(kernel, rows_count, cols_count),
        out_shape=(
            pltpu.VMEM(right.shape, f32),
            pltpu.VMEM(left.shape, f32),
            pltpu.VMEM((3, depth), f32),
        ),
        in_specs=[pl.BlockSpec(memory_space=pltpu.HBM)] * 6,
        out_specs=(pl.BlockSpec(memory_space=pltpu.VMEM),) * 3,
        scratch_shapes=[
            pltpu.VMEM((4, depth, share), f32),
            pltpu.VMEM(coupling.shape, f32),
            pltpu.VMEM(ladder.shape, ladder.dtype),
            pltpu.VMEM(ladder.shape[::-1], ladder.dtype),
            tiles(1),
            tiles(3),
            tiles(rows_count),
            tiles(cols_count),
            pltpu.VMEM((pack, 3, depth, LANES), f32),
            tiles(cols_count // pack),
            tiles(rows_count // pack),
            tiles(cols_count),
            tiles(rows_count),
            pltpu.VMEM((1, LANES), f32),
            pltpu.VMEM((devices // pack, LANES), f32),
            pltpu.SemaphoreType.DMA((6,)),
            pltpu.SemaphoreType.DMA((6,)),
            pltpu.SemaphoreType.DMA((6,)),
        ],
        compiler_params=pltpu.CompilerParams(
            collective_id=0, has_side_effects=True, vmem_limit_bytes=32 * 1024 * 1024
        ),
    )(*(pltpu.with_memory_space_constraint(x, pltpu.HBM) for x in (right, left, prev_right, prev_left, coupling, ladder)))
    return pl.pallas_call(
        store,
        out_shape=tuple(jax.ShapeDtypeStruct(x.shape, x.dtype) for x in results),
        in_specs=[pl.BlockSpec(memory_space=pltpu.VMEM)] * 3,
        out_specs=(pl.BlockSpec(memory_space=pltpu.HBM),) * 3,
        scratch_shapes=[pltpu.SemaphoreType.DMA((3,))],
        compiler_params=pltpu.CompilerParams(vmem_limit_bytes=1024 * 1024),
    )(*(pltpu.with_memory_space_constraint(x, pltpu.VMEM) for x in results))


def solution(mesh):
    vector = P(None, ("row", "col"))
    return jax.shard_map(
        functools.partial(local, mesh.shape["row"], mesh.shape["col"]),
        mesh=mesh,
        in_specs=(vector, vector, vector, vector, P(), P("row", "col")),
        out_specs=(vector, vector, P()),
        check_vma=False,
    )
```

profile of v0, /device:TPU:0, one launch (start us, length us, event | category | flops | bytes accessed | tf_op | source)
XLA Modules:
  0.0 20.4 jit_solution(6891784568224064299)
XLA Ops:
  0.6 19.2 %shard_map.85 = (f32[8,64]{1,0:T(8,128)S(1)}, f32[8,64]{1,0:T(8,128)S(1)}, f32[3,8]{1,0:T(4,128)S(1)}) custom-call(f32[8,64]{1,0:T(8,128)} %right_in.1, f32[8,64]{1,0:T(8,128)} %left_in.1, f32[8,64]{1,0:T(8,128)} %prev_right_in.1, f32[8,64]{1,0:T(8,128)} %prev_left_in.1, f32[2,8]{1,0:T(2,128)} %coupling_in.1, bf16[256,512]{1,0:T(8,128)(2,1)} %ladder_in.1), custom_call_target="tpu_custom_call" | custom-call | tf_op jit(solution)/shard_map/pallas_call | solution.py:372
  19.8 0.6 %shard_map.86 = (f32[8,64]{1,0:T(8,128)}, f32[8,64]{1,0:T(8,128)}, f32[3,8]{1,0:T(4,128)}) custom-call(f32[8,64]{1,0:T(8,128)S(1)} %get-tuple-element.6.a_in, f32[8,64]{1,0:T(8,128)S(1)} %get-tuple-element.7.b_in, f32[3,8]{1,0:T(4,128)S(1)} %get-tuple-element.8.c_in), custom_call_target="tpu_custom_call" | custom-call | tf_op jit(solution)/shard_map/pallas_call | solution.py:405
where the time goes:
time: 20.6 us; the launch traced here: 20.4 us
  Pallas kernels  19.8 us (96%)
  between operations  0.64 us (3%)
    pallas_call x1, Pallas kernels, local(): pl.pallas_call(functools.partial(kernel, rows_count, cols_count), out_sha...  19.2 us
    pallas_call x1, Pallas kernels, local(): pl.pallas_call(store, out_shape=tuple((jax.ShapeDtypeStruct(x.shape, x.dt...  0.63 us

commit v1 on v0

--- a/solution.py
+++ b/solution.py
@@ -9,6 +9,7 @@
 
 LOGICAL = pl.DeviceIdType.LOGICAL
 LANES = 128
+LAYERS = 4
 UNROLL_MOST = 32
 SMALLEST_SQUARE = 1e-12
 
@@ -68,6 +69,12 @@
     home_slot = lax.rem(me, rows_count)
     at_home = home_col == my_col
 
+    layers = LAYERS if rows_count % LAYERS == 0 else 1
+    span = rows_count // layers
+    layer = lax.div(my_row, span)
+    above = layer > lax.div(lax.div(my_col * rows_count, cols_count), span)
+    first_half = my_row < rows_count // 2
+
     groups = devices // pack
     my_group = lax.div(me, pack)
     my_sub = lax.rem(me, pack)
@@ -93,7 +100,8 @@
         return my_col * rows_count + lax.rem(home_slot + i, rows_count)
 
     def user(i):
-        return lax.rem(my_row + i, rows_count) * cols_count + home_col
+        step = jnp.where(first_half, rows_count - i, i)
+        return lax.rem(my_row + step, rows_count) * cols_count + home_col
 
     def unless_me(i, go):
         if i == 0:
@@ -106,14 +114,16 @@
     def greet(device):
         pl.semaphore_signal(barrier, inc=1, device_id=device, device_id_type=LOGICAL)
 
-    for i in range(cols_count - 1):
-        greet(peer(i))
     for load in loads[:2]:
         load.start()
     for i in range(rows_count):
         unless_me(i, lambda: greet(holder(i)))
-    for i in range(rows_count):
-        unless_me(i, lambda: greet(user(i)))
+    for i in range(cols_count - 1):
+        greet(peer(i))
+    for row in range(span, rows_count):
+        pl.when(row >= (layer + 1) * span)(
+            functools.partial(greet, row * cols_count + home_col)
+        )
     for load in loads[2:]:
         load.start()
 
@@ -146,7 +156,8 @@
     def _():
         right_got[pl.ds(home_slot, 1)] = right_own[None]
 
-    pl.semaphore_wait(barrier, 2 * rows_count + cols_count - 1 - 2 * at_home.astype(jnp.int32))
+    awaited = rows_count + cols_count - 1 - at_home.astype(jnp.int32)
+    pl.semaphore_wait(barrier, awaited + jnp.where(above, rows_count, 0))
 
     def send(src, dst, sems, device):
         pltpu.make_async_remote_copy(
@@ -158,10 +169,15 @@
             device_id_type=LOGICAL,
         ).start()
 
+    def send_right(i):
+        unless_me(i, lambda: send(mates_sent.at[0], right_got.at[home_slot], 0, user(i)))
+
+    for i in range(1, rows_count // 2):
+        send_right(i)
     for i in range(cols_count - 1):
         send(left_sent.at[0], left_got.at[my_col], 1, peer(i))
-    for i in (*range(1, rows_count), 0):
-        unless_me(i, lambda: send(mates_sent.at[0], right_got.at[home_slot], 0, user(i)))
+    for i in (*range(rows_count // 2, rows_count), 0):
+        send_right(i)
 
     for load in loads[2:]:
         load.wait()
@@ -189,12 +205,14 @@
     for i in range(rows_count // pack):
         left_part[i] = left_terms[:, i * LANES : (i + 1) * LANES]
 
-    for i in (*range(1, rows_count), 0):
-        chunk = lax.div(lax.rem(home_slot + i, rows_count), pack)
-        unless_me(
-            i, lambda: send(left_part.at[chunk], left_part_got.at[my_row], 2, holder(i))
-        )
-
+    def send_left_parts():
+        for i in (*range(1, rows_count), 0):
+            chunk = lax.div(lax.rem(home_slot + i, rows_count), pack)
+            unless_me(
+                i, lambda: send(left_part.at[chunk], left_part_got.at[my_row], 2, holder(i))
+            )
+
+    pl.when(above)(send_left_parts)
     for i in range(pack - 1):
         mate = me - my_sub + lax.rem(my_sub + i + 1, pack)
         send(mates_sent, mates_got.at[my_sub], 5, mate)
@@ -209,6 +227,7 @@
     def _():
         arrived(right_got, rows_count, recv_sem.at[0])
 
+    pl.when(jnp.logical_not(above))(send_left_parts)
     right_cols = joined(right_got, rows_count)
     right_terms = jnp.dot(
         right_cols.astype(jnp.bfloat16), ladder_turned[...], preferred_element_type=jnp.float32

time: 20.6 us -> 20.5 us (level)
  no operation moved by 1% of the time
where the time goes in v1:
time: 20.5 us; the launch traced here: 20.3 us
  Pallas kernels  19.6 us (96%)
  between operations  0.64 us (3%)
    pallas_call x1, Pallas kernels, local(): pl.pallas_call(functools.partial(kernel, rows_count, cols_count), out_sha...  19 us
    pallas_call x1, Pallas kernels, local(): pl.pallas_call(store, out_shape=tuple((jax.ShapeDtypeStruct(x.shape, x.dt...  0.63 us

profile of v1, /device:TPU:0, one launch (start us, length us, event | category | flops | bytes accessed | tf_op | source)
XLA Modules:
  0.0 20.3 jit_solution(8011899752263332594)
XLA Ops:
  0.6 19.0 %shard_map.85 = (f32[8,64]{1,0:T(8,128)S(1)}, f32[8,64]{1,0:T(8,128)S(1)}, f32[3,8]{1,0:T(4,128)S(1)}) custom-call(f32[8,64]{1,0:T(8,128)} %right_in.1, f32[8,64]{1,0:T(8,128)} %left_in.1, f32[8,64]{1,0:T(8,128)} %prev_right_in.1, f32[8,64]{1,0:T(8,128)} %prev_left_in.1, f32[2,8]{1,0:T(2,128)} %coupling_in.1, bf16[256,512]{1,0:T(8,128)(2,1)} %ladder_in.1), custom_call_target="tpu_custom_call" | custom-call | tf_op jit(solution)/shard_map/pallas_call | solution.py:391
  19.6 0.6 %shard_map.86 = (f32[8,64]{1,0:T(8,128)}, f32[8,64]{1,0:T(8,128)}, f32[3,8]{1,0:T(4,128)}) custom-call(f32[8,64]{1,0:T(8,128)S(1)} %get-tuple-element.6.a_in, f32[8,64]{1,0:T(8,128)S(1)} %get-tuple-element.7.b_in, f32[3,8]{1,0:T(4,128)S(1)} %get-tuple-element.8.c_in), custom_call_target="tpu_custom_call" | custom-call | tf_op jit(solution)/shard_map/pallas_call | solution.py:424

commit v2 on v1

--- a/solution.py
+++ b/solution.py
@@ -72,7 +72,7 @@
     layers = LAYERS if rows_count % LAYERS == 0 else 1
     span = rows_count // layers
     layer = lax.div(my_row, span)
-    above = layer > lax.div(lax.div(my_col * rows_count, cols_count), span)
+    below = layer < lax.div(lax.div(my_col * rows_count, cols_count), span)
     first_half = my_row < rows_count // 2
 
     groups = devices // pack
@@ -114,14 +114,15 @@
     def greet(device):
         pl.semaphore_signal(barrier, inc=1, device_id=device, device_id_type=LOGICAL)
 
+    for i in range(cols_count - 1):
+        greet(peer(i))
     for load in loads[:2]:
         load.start()
     for i in range(rows_count):
         unless_me(i, lambda: greet(holder(i)))
-    for i in range(cols_count - 1):
-        greet(peer(i))
-    for row in range(span, rows_count):
-        pl.when(row >= (layer + 1) * span)(
+    for row in range(rows_count):
+        is_me = jnp.logical_and(at_home, my_row == row)
+        pl.when(jnp.logical_and(row >= layer * span, jnp.logical_not(is_me)))(
             functools.partial(greet, row * cols_count + home_col)
         )
     for load in loads[2:]:
@@ -156,8 +157,8 @@
     def _():
         right_got[pl.ds(home_slot, 1)] = right_own[None]
 
-    awaited = rows_count + cols_count - 1 - at_home.astype(jnp.int32)
-    pl.semaphore_wait(barrier, awaited + jnp.where(above, rows_count, 0))
+    others = rows_count - at_home.astype(jnp.int32)
+    pl.semaphore_wait(barrier, cols_count - 1 + others + jnp.where(below, 0, others))
 
     def send(src, dst, sems, device):
         pltpu.make_async_remote_copy(
@@ -172,11 +173,9 @@
     def send_right(i):
         unless_me(i, lambda: send(mates_sent.at[0], right_got.at[home_slot], 0, user(i)))
 
-    for i in range(1, rows_count // 2):
-        send_right(i)
     for i in range(cols_count - 1):
         send(left_sent.at[0], left_got.at[my_col], 1, peer(i))
-    for i in (*range(rows_count // 2, rows_count), 0):
+    for i in (*range(1, rows_count), 0):
         send_right(i)
 
     for load in loads[2:]:
@@ -212,7 +211,7 @@
                 i, lambda: send(left_part.at[chunk], left_part_got.at[my_row], 2, holder(i))
             )
 
-    pl.when(above)(send_left_parts)
+    pl.when(jnp.logical_not(below))(send_left_parts)
     for i in range(pack - 1):
         mate = me - my_sub + lax.rem(my_sub + i + 1, pack)
         send(mates_sent, mates_got.at[my_sub], 5, mate)
@@ -227,7 +226,7 @@
     def _():
         arrived(right_got, rows_count, recv_sem.at[0])
 
-    pl.when(jnp.logical_not(above))(send_left_parts)
+    pl.when(below)(send_left_parts)
     right_cols = joined(right_got, rows_count)
     right_terms = jnp.dot(
         right_cols.astype(jnp.bfloat16), ladder_turned[...], preferred_element_type=jnp.float32

time: 20.5 us -> 20.4 us (level)
  no operation moved by 1% of the time
where the time goes in v2:
time: 20.4 us; the launch traced here: 20.2 us
  Pallas kernels  19.6 us (96%)
  between operations  0.64 us (3%)
    pallas_call x1, Pallas kernels, local(): pl.pallas_call(functools.partial(kernel, rows_count, cols_count), out_sha...  18.9 us
    pallas_call x1, Pallas kernels, local(): pl.pallas_call(store, out_shape=tuple((jax.ShapeDtypeStruct(x.shape, x.dt...  0.63 us

profile of v2, /device:TPU:0, one launch (start us, length us, event | category | flops | bytes accessed | tf_op | source)
XLA Modules:
  0.0 20.2 jit_solution(11457229634851529104)
XLA Ops:
  0.6 18.9 %shard_map.85 = (f32[8,64]{1,0:T(8,128)S(1)}, f32[8,64]{1,0:T(8,128)S(1)}, f32[3,8]{1,0:T(4,128)S(1)}) custom-call(f32[8,64]{1,0:T(8,128)} %right_in.1, f32[8,64]{1,0:T(8,128)} %left_in.1, f32[8,64]{1,0:T(8,128)} %prev_right_in.1, f32[8,64]{1,0:T(8,128)} %prev_left_in.1, f32[2,8]{1,0:T(2,128)} %coupling_in.1, bf16[256,512]{1,0:T(8,128)(2,1)} %ladder_in.1), custom_call_target="tpu_custom_call" | custom-call | tf_op jit(solution)/shard_map/pallas_call | solution.py:390
  19.6 0.6 %shard_map.86 = (f32[8,64]{1,0:T(8,128)}, f32[8,64]{1,0:T(8,128)}, f32[3,8]{1,0:T(4,128)}) custom-call(f32[8,64]{1,0:T(8,128)S(1)} %get-tuple-element.6.a_in, f32[8,64]{1,0:T(8,128)S(1)} %get-tuple-element.7.b_in, f32[3,8]{1,0:T(4,128)S(1)} %get-tuple-element.8.c_in), custom_call_target="tpu_custom_call" | custom-call | tf_op jit(solution)/shard_map/pallas_call | solution.py:423

commit v3 on v1

--- a/solution.py
+++ b/solution.py
@@ -42,7 +42,6 @@
     vectors_own,
     coupling_own,
     ladder_own,
-    ladder_turned,
     left_sent,
     mates_sent,
     right_got,
@@ -216,7 +215,6 @@
     for i in range(pack - 1):
         mate = me - my_sub + lax.rem(my_sub + i + 1, pack)
         send(mates_sent, mates_got.at[my_sub], 5, mate)
-    ladder_turned[...] = ladder_own[...].T
 
     @pl.when(at_home)
     def _():
@@ -229,8 +227,11 @@
 
     pl.when(jnp.logical_not(above))(send_left_parts)
     right_cols = joined(right_got, rows_count)
-    right_terms = jnp.dot(
-        right_cols.astype(jnp.bfloat16), ladder_turned[...], preferred_element_type=jnp.float32
+    right_terms = lax.dot_general(
+        right_cols.astype(jnp.bfloat16),
+        ladder_own[...],
+        (((1,), (1,)), ((), ())),
+        preferred_element_type=jnp.float32,
     )
     for i in range(cols_count // pack):
         right_part[i] = right_terms[:, i * LANES : (i + 1) * LANES]
@@ -401,7 +402,6 @@
             pltpu.VMEM((4, depth, share), f32),
             pltpu.VMEM(coupling.shape, f32),
             pltpu.VMEM(ladder.shape, ladder.dtype),
-            pltpu.VMEM(ladder.shape[::-1], ladder.dtype),
             tiles(1),
             tiles(3),
             tiles(rows_count),

time: 20.5 us -> 20.5 us (level)
  no operation moved by 1% of the time
where the time goes in v3:
time: 20.5 us; the launch traced here: 20.3 us
  Pallas kernels  19.6 us (96%)
  between operations  0.64 us (3%)
    pallas_call x1, Pallas kernels, local(): pl.pallas_call(functools.partial(kernel, rows_count, cols_count), out_sha...  19 us
    pallas_call x1, Pallas kernels, local(): pl.pallas_call(store, out_shape=tuple((jax.ShapeDtypeStruct(x.shape, x.dt...  0.63 us

profile of v3, /device:TPU:0, one launch (start us, length us, event | category | flops | bytes accessed | tf_op | source)
XLA Modules:
  0.0 20.3 jit_solution(3490976677014722576)
XLA Ops:
  0.6 19.0 %shard_map.85 = (f32[8,64]{1,0:T(8,128)S(1)}, f32[8,64]{1,0:T(8,128)S(1)}, f32[3,8]{1,0:T(4,128)S(1)}) custom-call(f32[8,64]{1,0:T(8,128)} %right_in.1, f32[8,64]{1,0:T(8,128)} %left_in.1, f32[8,64]{1,0:T(8,128)} %prev_right_in.1, f32[8,64]{1,0:T(8,128)} %prev_left_in.1, f32[2,8]{1,0:T(2,128)} %coupling_in.1, bf16[256,512]{1,0:T(8,128)(2,1)} %ladder_in.1), custom_call_target="tpu_custom_call" | custom-call | tf_op jit(solution)/shard_map/pallas_call | solution.py:392
  19.7 0.6 %shard_map.86 = (f32[8,64]{1,0:T(8,128)}, f32[8,64]{1,0:T(8,128)}, f32[3,8]{1,0:T(4,128)}) custom-call(f32[8,64]{1,0:T(8,128)S(1)} %get-tuple-element.6.a_in, f32[8,64]{1,0:T(8,128)S(1)} %get-tuple-element.7.b_in, f32[3,8]{1,0:T(4,128)S(1)} %get-tuple-element.8.c_in), custom_call_target="tpu_custom_call" | custom-call | tf_op jit(solution)/shard_map/pallas_call | solution.py:424

commit v4 on v2

--- a/solution.py
+++ b/solution.py
@@ -42,7 +42,6 @@
     vectors_own,
     coupling_own,
     ladder_own,
-    ladder_turned,
     left_sent,
     mates_sent,
     right_got,
@@ -114,10 +113,10 @@
     def greet(device):
         pl.semaphore_signal(barrier, inc=1, device_id=device, device_id_type=LOGICAL)
 
+    for load in loads[:2]:
+        load.start()
     for i in range(cols_count - 1):
         greet(peer(i))
-    for load in loads[:2]:
-        load.start()
     for i in range(rows_count):
         unless_me(i, lambda: greet(holder(i)))
     for row in range(rows_count):
@@ -215,7 +214,6 @@
     for i in range(pack - 1):
         mate = me - my_sub + lax.rem(my_sub + i + 1, pack)
         send(mates_sent, mates_got.at[my_sub], 5, mate)
-    ladder_turned[...] = ladder_own[...].T
 
     @pl.when(at_home)
     def _():
@@ -228,8 +226,11 @@
 
     pl.when(below)(send_left_parts)
     right_cols = joined(right_got, rows_count)
-    right_terms = jnp.dot(
-        right_cols.astype(jnp.bfloat16), ladder_turned[...], preferred_element_type=jnp.float32
+    right_terms = lax.dot_general(
+        right_cols.astype(jnp.bfloat16),
+        ladder_own[...],
+        (((1,), (1,)), ((), ())),
+        preferred_element_type=jnp.float32,
     )
     for i in range(cols_count // pack):
         right_part[i] = right_terms[:, i * LANES : (i + 1) * LANES]
@@ -400,7 +401,6 @@
             pltpu.VMEM((4, depth, share), f32),
             pltpu.VMEM(coupling.shape, f32),
             pltpu.VMEM(ladder.shape, ladder.dtype),
-            pltpu.VMEM(ladder.shape[::-1], ladder.dtype),
             tiles(1),
             tiles(3),
             tiles(rows_count),

time: 20.4 us -> 20.4 us (level)
  no operation moved by 1% of the time
where the time goes in v4:
time: 20.4 us; the launch traced here: 20.2 us
  Pallas kernels  19.6 us (96%)
  between operations  0.64 us (3%)
    pallas_call x1, Pallas kernels, local(): pl.pallas_call(functools.partial(kernel, rows_count, cols_count), out_sha...  18.9 us
    pallas_call x1, Pallas kernels, local(): pl.pallas_call(store, out_shape=tuple((jax.ShapeDtypeStruct(x.shape, x.dt...  0.63 us

profile of v4, /device:TPU:0, one launch (start us, length us, event | category | flops | bytes accessed | tf_op | source)
XLA Modules:
  0.0 20.2 jit_solution(10840078539507827492)
XLA Ops:
  0.6 18.9 %shard_map.85 = (f32[8,64]{1,0:T(8,128)S(1)}, f32[8,64]{1,0:T(8,128)S(1)}, f32[3,8]{1,0:T(4,128)S(1)}) custom-call(f32[8,64]{1,0:T(8,128)} %right_in.1, f32[8,64]{1,0:T(8,128)} %left_in.1, f32[8,64]{1,0:T(8,128)} %prev_right_in.1, f32[8,64]{1,0:T(8,128)} %prev_left_in.1, f32[2,8]{1,0:T(2,128)} %coupling_in.1, bf16[256,512]{1,0:T(8,128)(2,1)} %ladder_in.1), custom_call_target="tpu_custom_call" | custom-call | tf_op jit(solution)/shard_map/pallas_call | solution.py:391
  19.6 0.6 %shard_map.86 = (f32[8,64]{1,0:T(8,128)}, f32[8,64]{1,0:T(8,128)}, f32[3,8]{1,0:T(4,128)}) custom-call(f32[8,64]{1,0:T(8,128)S(1)} %get-tuple-element.6.a_in, f32[8,64]{1,0:T(8,128)S(1)} %get-tuple-element.7.b_in, f32[3,8]{1,0:T(4,128)S(1)} %get-tuple-element.8.c_in), custom_call_target="tpu_custom_call" | custom-call | tf_op jit(solution)/shard_map/pallas_call | solution.py:423
